TPU v7x, 512 devices: a whole 4x4x16 slice. The times are simulated.
512 devices in a mesh: img: 128 (over y, z, core), tp: 4 (over x).
Axes of the slice: x: 4, y: 4, z: 16, core: 2. Of those that a mesh axis runs over, the one named last changes fastest.
Arguments:
- encoded: bfloat16 [2048, 8, 1024], P('img'), may hold values from -6 to 6
- pair_images: int32 [4096, 2], replicated, may hold values from 0 to 2047, as said below
- embed_w: bfloat16 [1024, 768], replicated, may hold values from -0.1875 to 0.1875
- gain_query: bfloat16 [768], replicated, may hold values from 0.099609375 to 1.8984375
- gain_key: bfloat16 [768], replicated, may hold values from 0.099609375 to 1.8984375
- gain_out: bfloat16 [768], replicated, may hold values from 0.099609375 to 1.8984375
- w_query: bfloat16 [768, 768], P(None, 'tp'), may hold values from -3 to 3
- w_key: bfloat16 [768, 768], P(None, 'tp'), may hold values from -3 to 3
- w_value: bfloat16 [768, 768], P(None, 'tp'), may hold values from -0.21875 to 0.21875
- w_out: bfloat16 [768, 768], P('tp'), may hold values from -0.21875 to 0.21875
- head_w: bfloat16 [768, 1024], P('tp'), may hold values from -0.21875 to 0.21875
Outputs:
- pointmaps: bfloat16 [2048, 8, 1024], P('img', None, 'tp')
Inputs may be any that keep to these rules, and one draw needn't show every extreme that they name: `pair_images`: A global image id is owner index times 16 plus the position among that owner's images. Worker w runs pairs w * 32 to (w + 1) * 32 - 1. The 64 images named in one worker's pairs are all different, and at most 1 of them lie on one owner; in every draw some owner holds exactly 1 of them. The two images of a pair lie on different owners.
All inputs are finite; a program needn't handle non-finite values.
Results may differ from a plain program's by a relative error of at most 0.02.
Values may be sent and summed in bfloat16 or wider, within the bound.
A program may use at most 64 MiB of HBM per device.

v0:
```python
import jax
import jax.numpy as jnp
from jax import lax
from jax.sharding import PartitionSpec as P

HEAD_DIM = 64


def layer_norm(values, gain):
    center = values - jnp.mean(values, axis=-1, keepdims=True)
    spread = jnp.mean(center * center, axis=-1, keepdims=True)
    return center * lax.rsqrt(spread + 1e-06) * gain.astype(jnp.float32)


def select_rows(selector, source):
    flat = source.reshape(source.shape[0], -1)
    picked = jnp.dot(
        selector.astype(jnp.bfloat16), flat, preferred_element_type=jnp.float32
    ).astype(jnp.bfloat16)
    return picked.reshape((selector.shape[0],) + source.shape[1:])


def shards(
    encoded,
    pair_images,
    embed_w,
    gain_query,
    gain_key,
    gain_out,
    w_query,
    w_key,
    w_value,
    w_out,
    head_w,
):
    owner_count = lax.axis_size("img")
    owner_self = lax.axis_index("img")
    group_count = lax.axis_size("tp")
    group_self = lax.axis_index("tp")
    images_here = encoded.shape[0]
    tokens_img = encoded.shape[1]
    width = embed_w.shape[1]
    group_w = width // group_count
    view_count = pair_images.shape[0] // owner_count * 2
    slot_cap = max(1, view_count // owner_count)
    table = pair_images.reshape(owner_count, view_count)
    view_index = jnp.arange(view_count, dtype=jnp.int32)
    before = view_index[:, None] < view_index[None, :]
    owner_table = table // images_here
    hits = owner_table == owner_self
    rank_all = jnp.sum((hits[:, :, None] & before[None, :, :]).astype(jnp.int32), axis=1)
    slot_hot = (
        hits[:, :, None]
        & (rank_all[:, :, None] == jnp.arange(slot_cap, dtype=jnp.int32)[None, None, :])
    ).astype(jnp.float32)
    positions = jnp.arange(images_here, dtype=jnp.int32)
    image_hot = ((table % images_here)[:, :, None] == positions[None, None, :]).astype(jnp.float32)
    outgoing = jnp.einsum("wvk,wvi->wki", slot_hot, image_hot).reshape(
        owner_count * slot_cap, images_here
    )
    my_ids = lax.dynamic_index_in_dim(table, owner_self, 0, keepdims=False)
    my_owners = my_ids // images_here
    same_owner = my_owners[:, None] == my_owners[None, :]
    my_rank = jnp.sum((same_owner & before).astype(jnp.int32), axis=0)
    slot_of = my_owners * slot_cap + my_rank
    incoming = (
        slot_of[:, None] == jnp.arange(owner_count * slot_cap, dtype=jnp.int32)[None, :]
    ).astype(jnp.float32)
    enc_width = encoded.shape[2] // group_count
    local = lax.dynamic_slice_in_dim(encoded, group_self * enc_width, enc_width, 2)
    received = lax.all_to_all(
        select_rows(outgoing, local), "img", split_axis=0, concat_axis=0, tiled=True
    )
    view_part = select_rows(incoming, received)
    enc_views = lax.all_gather(view_part, "tp", axis=2, tiled=True)
    views = jnp.dot(enc_views, embed_w, preferred_element_type=jnp.float32).astype(jnp.bfloat16)
    base_norm = layer_norm(views.astype(jnp.float32), jnp.ones((width,), jnp.float32))
    swapped = base_norm.reshape(view_count // 2, 2, tokens_img, width)[:, ::-1].reshape(
        view_count, tokens_img, width
    )
    normed_q = (base_norm * gain_query.astype(jnp.float32)).astype(jnp.bfloat16)
    normed_k = (swapped * gain_key.astype(jnp.float32)).astype(jnp.bfloat16)
    query = (
        jnp.dot(normed_q, w_query, preferred_element_type=jnp.float32) * HEAD_DIM ** (-0.5)
    ).astype(jnp.bfloat16)
    keys = jnp.dot(normed_k, w_key, preferred_element_type=jnp.float32).astype(jnp.bfloat16)
    values = jnp.dot(normed_k, w_value, preferred_element_type=jnp.float32).astype(jnp.bfloat16)
    heads_here = group_w // HEAD_DIM
    query = query.reshape(view_count, tokens_img, heads_here, HEAD_DIM)
    keys = keys.reshape(view_count, tokens_img, heads_here, HEAD_DIM)
    values = values.reshape(view_count, tokens_img, heads_here, HEAD_DIM)
    scores = jnp.einsum("vqhd,vkhd->vhqk", query, keys, preferred_element_type=jnp.float32)
    weights = jax.nn.softmax(scores, axis=-1).astype(jnp.bfloat16)
    attended = jnp.einsum(
        "vhqk,vkhd->vqhd", weights, values, preferred_element_type=jnp.float32
    ).astype(jnp.bfloat16)
    attended = attended.reshape(view_count, tokens_img, group_w)
    partial_mix = jnp.dot(attended, w_out, preferred_element_type=jnp.float32)
    mixed = lax.psum(partial_mix.astype(jnp.bfloat16), "tp").astype(jnp.float32)
    hidden = views.astype(jnp.float32) + mixed
    normed = layer_norm(hidden, gain_out).astype(jnp.bfloat16)
    share = lax.dynamic_slice_in_dim(normed, group_self * group_w, group_w, 2)
    returned = lax.all_to_all(
        select_rows(incoming.T, share), "img", split_axis=0, concat_axis=0, tiled=True
    )
    flat_back = returned.reshape(owner_count * slot_cap, -1)
    summed = jnp.dot(outgoing.T.astype(jnp.bfloat16), flat_back, preferred_element_type=jnp.float32)
    summed = summed.astype(jnp.bfloat16).reshape(images_here, tokens_img, group_w)
    head_terms = jnp.dot(summed, head_w, preferred_element_type=jnp.float32)
    return lax.psum_scatter(head_terms.astype(jnp.bfloat16), "tp", scatter_dimension=2, tiled=True)


def solution(mesh):
    placed = (
        P("img", None, None),
        P(),
        P(),
        P(),
        P(),
        P(),
        P(None, "tp"),
        P(None, "tp"),
        P(None, "tp"),
        P("tp", None),
        P("tp", None),
    )
    return jax.shard_map(
        shards, mesh=mesh, in_specs=placed, out_specs=P("img", None, "tp"), check_vma=False
    )
```

profile of v0, /device:TPU:8, one launch (start us, length us, event | category | flops | bytes accessed | tf_op | source)
XLA Modules:
  0.0 263.7 jit_solution(15759082420801121636)
XLA Ops:
  6.6 1.0 constant_dynamic-slice_fusion
  7.5 2.8 %copy.40 = s32[4096,2]{1,0:T(8,128)} copy(s32[4096,2]{0,1:T(2,128)} %param.12) | data formatting | bytes 65536 | tf_op args[1]
  10.3 3.2 %reshape.185 = s32[128,64]{1,0:T(8,128)S(1)} reshape(s32[4096,2]{1,0:T(8,128)} %copy.40) | data formatting | bytes 65536 | tf_op jit(solution)/shard_map/reshape | solution.py:46
  15.8 19.6 %all-to-all-start = ((bf16[128,8,256]{2,1,0:T(8,128)(2,1)}), bf16[128,8,256]{2,1,0:T(8,128)(2,1)S(1)}, u32[]{:S(2)}, u32[]{:S(2)}) async-start(bf16[128,8,256]{2,1,0:T(8,128)(2,1)} %bitcast.20), calls=%async_computation | async-start | bytes 1048576 | tf_op jit(solution)/shard_map/all_to_all | solution.py:71
  35.7 33.4 %all-to-all-done = bf16[128,8,256]{2,1,0:T(8,128)(2,1)S(1)} async-done(((bf16[128,8,256]{2,1,0:T(8,128)(2,1)}), bf16[128,8,256]{2,1,0:T(8,128)(2,1)S(1)}, u32[]{:S(2)}, u32[]{:S(2)}) %all-to-all-start) | async-done | bytes 524320 | tf_op jit(solution)/shard_map/all_to_all | solution.py:71
  70.5 24.9 %all-gather.2.cloned.1.call-done = bf16[64,8,1024]{2,1,0:T(8,128)(2,1)} async-done(((bf16[64,8,256]{2,1,0:T(8,128)(2,1)}), bf16[64,8,1024]{2,1,0:T(8,128)(2,1)}) %all-gather.2.cloned.1.call-update) | async-done | bytes 1048592 | tf_op jit(solution)/shard_map/all_gather | solution.py:75
  95.4 2.3 convert_reduce_fusion
  98.7 1.4 fusion.1
  100.2 2.7 %rev.3 = f32[32,2,8,768]{3,2,1,0:T(8,128)} reverse(f32[32,2,8,768]{3,2,1,0:T(8,128)} %bitcast.71), dimensions={1} | reverse | bytes 3145728 | tf_op jit(solution)/shard_map/rev | solution.py:78
  102.8 1.6 fusion.4
  104.4 1.1 convolution_convert_fusion.8
  105.5 1.2 copy.45
  106.7 1.0 copy.50
  107.7 2.1 fusion.14
  109.8 1.2 copy.46
  111.1 1.0 copy.48
  112.0 2.1 convolution_convert_fusion.7
  114.1 1.2 copy.47
  117.4 1.9 fusion.15
  120.3 1.3 convolution_convert_fusion.4
  121.7 60.8 %all-reduce.2.cloned.1.call-done = bf16[64,8,768]{2,1,0:T(8,128)(2,1)} async-done(((bf16[64,8,768]{2,1,0:T(8,128)(2,1)}), bf16[64,8,768]{2,1,0:T(8,128)(2,1)}) %all-reduce.2.cloned.1.call-update) | async-done | bytes 786448 | tf_op jit(solution)/shard_map/psum | solution.py:99
  182.5 1.5 fusion.8
  185.9 50.0 %all_to_all.10 = bf16[128,8,192]{2,1,0:T(8,128)(2,1)S(1)} all-to-all(bf16[128,8,192]{2,1,0:T(8,128)(2,1)S(1)} %copy.55), channel_id=1, replica_groups=mesh['img'=128,'tp'=4] {'img'}, dimensions={0} | all-to-all | bytes 786432 | tf_op jit(solution)/shard_map/all_to_all | solution.py:103
  237.7 19.5 %reduce-scatter.2.cloned.1.call-done = bf16[16,8,256]{2,1,0:T(8,128)(2,1)} async-done(((bf16[16,8,1024]{2,1,0:T(8,128)(2,1)}), bf16[16,8,256]{2,1,0:T(8,128)(2,1)}) %reduce-scatter.2.cloned.1.call-update) | async-done | bytes 65552 | tf_op jit(solution)/shard_map/reduce_scatter | solution.py:110
  (77 shorter events, 11.5 us)
Async XLA Ops:
  6.5 88.9 %copy-start = (bf16[1024,768]{1,0:T(8,128)(2,1)S(1)}, bf16[1024,768]{1,0:T(8,128)(2,1)}, u32[]{:S(2)}) copy-start(bf16[1024,768]{1,0:T(8,128)(2,1)} %param.13) | copy-start | bytes 4718596
  14.6 1.2 copy-start.9
  15.8 53.3 %all-to-all-start = ((bf16[128,8,256]{2,1,0:T(8,128)(2,1)}), bf16[128,8,256]{2,1,0:T(8,128)(2,1)S(1)}, u32[]{:S(2)}, u32[]{:S(2)}) async-start(bf16[128,8,256]{2,1,0:T(8,128)(2,1)} %bitcast.20), calls=%async_computation | async-start | bytes 1048576 | tf_op jit(solution)/shard_map/all_to_all | solution.py:71
  35.4 35.1 %copy-start.12 = (bf16[768]{0:T(1024)(128)(2,1)S(1)}, bf16[768]{0:T(1024)(128)(2,1)}, u32[]{:S(2)}) copy-start(bf16[768]{0:T(1024)(128)(2,1)} %param.15) | copy-start | bytes 4612
  35.4 35.1 %copy-start.13 = (bf16[768]{0:T(1024)(128)(2,1)S(1)}, bf16[768]{0:T(1024)(128)(2,1)}, u32[]{:S(2)}) copy-start(bf16[768]{0:T(1024)(128)(2,1)} %param.14) | copy-start | bytes 4612
  35.4 60.0 %all-gather.2.cloned.1.call-start = ((), (), s32[]{:S(2)}) async-start(), calls=%async_computation.3 | async-start | bytes 1310720 | tf_op jit(solution)/shard_map/all_gather | solution.py:75
  70.2 112.3 %all-reduce.2.cloned.1.call-start = ((), (), s32[]{:S(2)}) async-start(), calls=%async_computation.4 | async-start | bytes 1572864 | tf_op jit(solution)/shard_map/psum | solution.py:99
  97.7 2.5 copy-start.6
  98.1 0.6 copy-start.11
  102.8 1.6 copy-start.7
  112.0 3.6 %copy-start.2 = (bf16[64,8,3,64]{3,1,2,0:T(8,128)(2,1)S(1)}, bf16[64,8,3,64]{3,1,2,0:T(8,128)(2,1)}, u32[]{:S(2)}) copy-start(bf16[64,8,3,64]{3,1,2,0:T(8,128)(2,1)} %copy.48) | copy-start | bytes 589828
  115.6 1.7 copy-start.4
  116.0 0.9 copy-start.3
  119.3 1.0 copy-start.8
  119.6 2.0 copy-start.14
  121.6 135.6 %reduce-scatter.2.cloned.1.call-start = ((), (), s32[]{:S(2)}) async-start(), calls=%async_computation.5 | async-start | bytes 327680 | tf_op jit(solution)/shard_map/reduce_scatter | solution.py:110
  182.5 1.5 copy-start.1
  185.5 50.9 %copy-start.10 = (bf16[128,16]{1,0:T(8,128)(2,1)S(1)}, bf16[128,16]{1,0:T(8,128)(2,1)}, u32[]{:S(2)}) copy-start(bf16[128,16]{1,0:T(8,128)(2,1)} %copy-done.9) | copy-start | bytes 12292
  185.5 51.3 %copy-start.5 = (bf16[192,1024]{1,0:T(8,128)(2,1)S(1)}, bf16[192,1024]{1,0:T(8,128)(2,1)}, u32[]{:S(2)}) copy-start(bf16[192,1024]{1,0:T(8,128)(2,1)} %param.21) | copy-start | bytes 1179652
Sparse Core Ops, SparseCore 0:
  70.4 25.0 all-gather.1
  121.7 60.7 all-reduce.1
  237.8 19.2 reduce-scatter.1
where the time goes:
time: 264 us
  waiting for transfers between devices  139 us (53%)
  blocking collectives  50 us (19%)
  local copies, waits for them, and re-layouts  21.4 us (8%)
  starting transfers between devices  19.9 us (8%)
  between operations  13.5 us (5%)
  matrix products  13 us (5%)
  other arithmetic  7.15 us (3%)
    psum x1, waiting for transfers between devices, shards(): mixed = lax.psum(partial_mix.astype(jnp.bfloat16), 'tp').astype(jnp.float32)  60.8 us
    all_to_all x1, blocking collectives, shards(): lax.all_to_all(select_rows(incoming.T, share), 'img', split_axis=0, conca...  50 us
    all_to_all x1, waiting for transfers between devices, shards(): lax.all_to_all(select_rows(outgoing, local), 'img', split_axis=0, concat_...  33.4 us
    all_gather x1, waiting for transfers between devices, shards(): enc_views = lax.all_gather(view_part, 'tp', axis=2, tiled=True)  24.9 us
    all_to_all x1, starting transfers between devices, shards(): lax.all_to_all(select_rows(outgoing, local), 'img', split_axis=0, concat_...  19.6 us
    reduce_scatter x1, waiting for transfers between devices, shards(): lax.psum_scatter(head_terms.astype(jnp.bfloat16), 'tp', scatter_dimension...  19.5 us
    unnamed x35, local copies, waits for them, and re-layouts  6.45 us
  transfers between devices with their start and end apart: 4, of which 4 were waited for; matrix products, arithmetic and copies ran while one was open for 0% of the time, Pallas kernels for 0%

commit v1 on v0

--- a/solution.py
+++ b/solution.py
@@ -96,7 +96,9 @@
     ).astype(jnp.bfloat16)
     attended = attended.reshape(view_count, tokens_img, group_w)
     partial_mix = jnp.dot(attended, w_out, preferred_element_type=jnp.float32)
-    mixed = lax.psum(partial_mix.astype(jnp.bfloat16), "tp").astype(jnp.float32)
+    mixed = jnp.sum(lax.all_gather(partial_mix.astype(jnp.bfloat16), "tp"), axis=0).astype(
+        jnp.float32
+    )
     hidden = views.astype(jnp.float32) + mixed
     normed = layer_norm(hidden, gain_out).astype(jnp.bfloat16)
     share = lax.dynamic_slice_in_dim(normed, group_self * group_w, group_w, 2)

time: 264 us -> 248 us (0.939)
  waiting for transfers between devices: 139 us -> 125 us
  local copies, waits for them, and re-layouts: 21.4 us -> 17.7 us
    psum x1 -> x0, waiting for transfers between devices: 60.8 us -> none  [shards(): mixed = lax.psum(partial_mix.astype(jnp.bfloat16), 'tp').astype(jnp.float32)]
    all_gather x0 -> x1, waiting for transfers between devices: none -> 48.3 us  [shards(): lax.all_gather(partial_mix.astype(jnp.bfloat16), 'tp')]
    reduce_sum x0 -> x1, other arithmetic: none -> 2.79 us  [shards(): jnp.sum(lax.all_gather(partial_mix.astype(jnp.bfloat16), 'tp'), axis=0)]
    unnamed x35 -> x27, local copies, waits for them, and re-layouts: 6.45 us -> 4.73 us
where the time goes in v1:
time: 248 us
  waiting for transfers between devices  125 us (50%)
  blocking collectives  50 us (20%)
  starting transfers between devices  19.9 us (8%)
  local copies, waits for them, and re-layouts  17.7 us (7%)
  between operations  13.5 us (5%)
  matrix products  11.8 us (5%)
  other arithmetic  9.38 us (4%)
    all_to_all x1, blocking collectives, shards(): lax.all_to_all(select_rows(incoming.T, share), 'img', split_axis=0, conca...  50 us
    all_gather x1, waiting for transfers between devices, shards(): lax.all_gather(partial_mix.astype(jnp.bfloat16), 'tp')  48.3 us
    all_to_all x1, waiting for transfers between devices, shards(): lax.all_to_all(select_rows(outgoing, local), 'img', split_axis=0, concat_...  33.4 us
    all_gather x1, waiting for transfers between devices, shards(): enc_views = lax.all_gather(view_part, 'tp', axis=2, tiled=True)  24.9 us
    all_to_all x1, starting transfers between devices, shards(): lax.all_to_all(select_rows(outgoing, local), 'img', split_axis=0, concat_...  19.6 us
    reduce_scatter x1, waiting for transfers between devices, shards(): lax.psum_scatter(head_terms.astype(jnp.bfloat16), 'tp', scatter_dimension...  18.8 us
  transfers between devices with their start and end apart: 4, of which 4 were waited for; matrix products, arithmetic and copies ran while one was open for 0% of the time, Pallas kernels for 0%

profile of v1, /device:TPU:8, one launch (start us, length us, event | category | flops | bytes accessed | tf_op | source)
XLA Modules:
  0.0 247.7 jit_solution(17995958238662863137)
XLA Ops:
  6.6 2.9 %copy.40 = s32[4096,2]{1,0:T(8,128)} copy(s32[4096,2]{0,1:T(2,128)} %param.12) | data formatting | bytes 65536 | tf_op args[1]
  9.4 3.2 %reshape.185 = s32[128,64]{1,0:T(8,128)S(1)} reshape(s32[4096,2]{1,0:T(8,128)} %copy.40) | data formatting | bytes 65536 | tf_op jit(solution)/shard_map/reshape | solution.py:46
  13.8 0.9 constant_dynamic-slice_fusion
  14.9 0.9 copy.65
  15.8 19.6 %all-to-all-start = ((bf16[128,8,256]{2,1,0:T(8,128)(2,1)}), bf16[128,8,256]{2,1,0:T(8,128)(2,1)S(1)}, u32[]{:S(2)}, u32[]{:S(2)}) async-start(bf16[128,8,256]{2,1,0:T(8,128)(2,1)} %bitcast.21), calls=%async_computation | async-start | bytes 1048576 | tf_op jit(solution)/shard_map/all_to_all | solution.py:71
  35.7 33.4 %all-to-all-done = bf16[128,8,256]{2,1,0:T(8,128)(2,1)S(1)} async-done(((bf16[128,8,256]{2,1,0:T(8,128)(2,1)}), bf16[128,8,256]{2,1,0:T(8,128)(2,1)S(1)}, u32[]{:S(2)}, u32[]{:S(2)}) %all-to-all-start) | async-done | bytes 524320 | tf_op jit(solution)/shard_map/all_to_all | solution.py:71
  70.5 24.9 %all-gather.4.cloned.1.call-done = bf16[64,8,1024]{2,1,0:T(8,128)(2,1)} async-done(((bf16[64,8,256]{2,1,0:T(8,128)(2,1)}), bf16[64,8,1024]{2,1,0:T(8,128)(2,1)}) %all-gather.4.cloned.1.call-update) | async-done | bytes 1048592 | tf_op jit(solution)/shard_map/all_gather | solution.py:75
  95.4 2.3 convert_reduce_fusion
  98.1 1.4 fusion.1
  100.3 1.0 copy.48
  101.3 2.7 %rev.3 = f32[32,2,8,768]{3,2,1,0:T(8,128)} reverse(f32[32,2,8,768]{3,2,1,0:T(8,128)} %bitcast.72), dimensions={1} | reverse | bytes 3145728 | tf_op jit(solution)/shard_map/rev | solution.py:78
  103.9 1.6 fusion.4
  105.5 1.1 convolution_convert_fusion.7
  106.6 1.2 copy.47
  107.8 1.0 copy.49
  108.8 1.5 fusion.36
  110.3 1.1 fusion.35
  112.4 2.0 fusion.15
  115.0 2.2 convolution_convert_fusion.4
  117.4 48.3 %all-gather.6.cloned.1.call-done = bf16[256,8,768]{2,1,0:T(8,128)(2,1)} async-done(((bf16[64,8,768]{2,1,0:T(8,128)(2,1)}), bf16[256,8,768]{2,1,0:T(8,128)(2,1)}) %all-gather.6.cloned.1.call-update) | async-done | bytes 3145744 | tf_op jit(solution)/shard_map/all_gather | solution.py:99
  165.7 2.8 %reduce_sum.80 = bf16[64,8,768]{2,1,0:T(8,128)(2,1)S(1)} reduce(bf16[4,64,8,768]{3,2,1,0:T(8,128)(2,1)} %bitcast.73, bf16[]{:T(256)} %constant.75.clone.1), dimensions={0}, to_apply=%region_6.7 | reduce | flops 1179648 | bytes 3932162 | tf_op jit(solution)/shard_map/reduce_sum | solution.py:99
  170.6 50.0 %all_to_all.10 = bf16[128,8,192]{2,1,0:T(8,128)(2,1)S(1)} all-to-all(bf16[128,8,192]{2,1,0:T(8,128)(2,1)S(1)} %copy.55), channel_id=1, replica_groups=mesh['img'=128,'tp'=4] {'img'}, dimensions={0} | all-to-all | bytes 786432 | tf_op jit(solution)/shard_map/all_to_all | solution.py:105
  221.5 0.9 convolution_convert_fusion.6
  222.4 18.8 %reduce-scatter.2.cloned.1.call-done = bf16[16,8,256]{2,1,0:T(8,128)(2,1)} async-done(((bf16[16,8,1024]{2,1,0:T(8,128)(2,1)}), bf16[16,8,256]{2,1,0:T(8,128)(2,1)}) %reduce-scatter.2.cloned.1.call-update) | async-done | bytes 65552 | tf_op jit(solution)/shard_map/reduce_scatter | solution.py:112
  (70 shorter events, 8.6 us)
Async XLA Ops:
  6.5 88.9 %copy-start = (bf16[1024,768]{1,0:T(8,128)(2,1)S(1)}, bf16[1024,768]{1,0:T(8,128)(2,1)}, u32[]{:S(2)}) copy-start(bf16[1024,768]{1,0:T(8,128)(2,1)} %param.13) | copy-start | bytes 4718596
  13.7 2.1 copy-start.5
  15.8 53.2 %all-to-all-start = ((bf16[128,8,256]{2,1,0:T(8,128)(2,1)}), bf16[128,8,256]{2,1,0:T(8,128)(2,1)S(1)}, u32[]{:S(2)}, u32[]{:S(2)}) async-start(bf16[128,8,256]{2,1,0:T(8,128)(2,1)} %bitcast.21), calls=%async_computation | async-start | bytes 1048576 | tf_op jit(solution)/shard_map/all_to_all | solution.py:71
  35.4 35.1 %copy-start.7 = (bf16[768]{0:T(1024)(128)(2,1)S(1)}, bf16[768]{0:T(1024)(128)(2,1)}, u32[]{:S(2)}) copy-start(bf16[768]{0:T(1024)(128)(2,1)} %param.14) | copy-start | bytes 4612
  35.4 35.1 %copy-start.8 = (bf16[768]{0:T(1024)(128)(2,1)S(1)}, bf16[768]{0:T(1024)(128)(2,1)}, u32[]{:S(2)}) copy-start(bf16[768]{0:T(1024)(128)(2,1)} %param.15) | copy-start | bytes 4612
  35.5 60.0 %all-gather.4.cloned.1.call-start = ((), (), s32[]{:S(2)}) async-start(), calls=%async_computation.3 | async-start | bytes 1310720 | tf_op jit(solution)/shard_map/all_gather | solution.py:75
  70.3 95.4 %all-gather.6.cloned.1.call-start = ((), (), s32[]{:S(2)}) async-start(), calls=%async_computation.5 | async-start | bytes 3932160 | tf_op jit(solution)/shard_map/all_gather | solution.py:99
  97.7 1.8 copy-start.10
  103.9 1.6 copy-start.3
  108.8 2.7 %copy-start.4 = (bf16[768,192]{0,1:T(8,128)(2,1)S(1)}, bf16[768,192]{0,1:T(8,128)(2,1)}, u32[]{:S(2)}) copy-start(bf16[768,192]{0,1:T(8,128)(2,1)} %param.19) | copy-start | bytes 884740
  110.3 1.2 copy-start.1
  114.7 2.6 %copy-start.9 = (bf16[768]{0:T(1024)(128)(2,1)S(1)}, bf16[768]{0:T(1024)(128)(2,1)}, u32[]{:S(2)}) copy-start(bf16[768]{0:T(1024)(128)(2,1)} %param.16) | copy-start | bytes 4612
  117.2 124.0 %reduce-scatter.2.cloned.1.call-start = ((), (), s32[]{:S(2)}) async-start(), calls=%async_computation.4 | async-start | bytes 327680 | tf_op jit(solution)/shard_map/reduce_scatter | solution.py:112
  170.2 50.9 %copy-start.6 = (bf16[128,16]{1,0:T(8,128)(2,1)S(1)}, bf16[128,16]{1,0:T(8,128)(2,1)}, u32[]{:S(2)}) copy-start(bf16[128,16]{1,0:T(8,128)(2,1)} %copy-done.5) | copy-start | bytes 12292
  170.2 51.3 %copy-start.2 = (bf16[192,1024]{1,0:T(8,128)(2,1)S(1)}, bf16[192,1024]{1,0:T(8,128)(2,1)}, u32[]{:S(2)}) copy-start(bf16[192,1024]{1,0:T(8,128)(2,1)} %param.21) | copy-start | bytes 1179652
Sparse Core Ops, SparseCore 0:
  70.4 25.0 all-gather.3
  117.4 48.2 all-gather.5
  222.5 18.6 reduce-scatter.1
